TPU v7x, 32 devices: a whole 2x2x4 slice. The times are simulated.
32 devices in a mesh: expert: 4 (over y, x), fsdp: 8 (over z, core).
Axes of the slice: x: 2, y: 2, z: 4, core: 2. Of those that a mesh axis runs over, the one named last changes fastest.
Arguments:
- tokens: bfloat16 [4608, 2048], P(('expert', 'fsdp')), may hold values from -6 to 6
- expert_ids: int32 [4608, 6], P(('expert', 'fsdp')), may hold values from 0 to 15, as said below
- combine: float32 [4608, 6], P(('expert', 'fsdp')), may hold values from 0.05 to 1
- gate_weight: bfloat16 [16, 1408, 2048], P('expert', 'fsdp'), may hold values from -0.125 to 0.125
- up_weight: bfloat16 [16, 1408, 2048], P('expert', 'fsdp'), may hold values from -0.125 to 0.125
- down_weight: bfloat16 [16, 1408, 2048], P('expert', 'fsdp'), may hold values from -0.15625 to 0.15625
Outputs:
- mixed: bfloat16 [4608, 2048], P(('expert', 'fsdp'))
Inputs may be any that keep to these rules, and one draw needn't show every extreme that they name: `expert_ids`: each row names 6 different experts. Within the 144 rows of each device no expert is named more than 72 times, and one and the same expert is named exactly 72 times by the rows of every device.
All inputs are finite; a program needn't handle non-finite values.
Results may differ from a plain program's by a relative error of at most 0.0058.
Values may be sent and summed in bfloat16 or wider, within the bound.
No kernel may reach another device: no remote copies, remote signals or barrier semaphores. Data moves between devices by JAX's collectives and lax.ppermute only.
A program may use at most 128 MiB of HBM per device.

v0:
```python
import functools

import jax
import jax.numpy as jnp
from jax import lax
from jax.experimental import pallas as pl
from jax.experimental.pallas import tpu as pltpu
from jax.sharding import Mesh, PartitionSpec as P

AXES = ("e_hi", "e_lo", "line", "core")
LANES = 128
TILE = 256


def tiles(extent, size=TILE):
    return [(at, min(size, extent - at)) for at in range(0, extent, size)]


def ffn_kernel(ny, nx, experts, per_group, *refs):
    place, refs = refs[0], refs[1:]
    first, refs = refs[0], refs[1:]
    near, refs = refs[: nx + ny - 2], refs[nx + ny - 2 :]
    left, right, refs = refs[: ny - 1], refs[ny - 1 : ny + nx - 2], refs[ny + nx - 2 :]
    weights, refs = refs[:6], refs[6:]
    send_a, keep_a, send_b, keep_b = refs[:4]
    rows, hidden, row_sem = refs[4:]
    count, depth = rows.shape[0], weights[0].shape[1]
    half = depth // 2
    units = weights[0].shape[0]
    tok = count // (ny * nx)
    group = place[0]

    row_copies = []

    def bring(source, from_row, block, low):
        cols = pl.ds(0, half) if low else pl.ds(half, rows.shape[1] - half)
        from_cols = cols if source.shape[1] == rows.shape[1] else pl.ds(0, source.shape[1])
        row_copies.append(
            pltpu.make_async_copy(
                source.at[pl.ds(from_row, tok), from_cols],
                rows.at[pl.ds(block * tok, tok), cols],
                row_sem.at[len(row_copies)],
            )
        )

    for jy in range(ny):
        for jx in range(nx):
            block = jy * nx + jx
            if jy:
                bring(left[jy - 1], jx * tok, block, True)
            else:
                bring(near[jx - 1] if jx else first, 0, block, True)
            if jx:
                bring(right[jx - 1], jy * tok, block, False)
            else:
                bring(near[nx - 1 + jy - 1] if jy else first, 0, block, False)
    for copy in row_copies:
        copy.start()
    for copy in row_copies:
        copy.wait()

    extra = rows[:, depth:].astype(jnp.float32)
    lane = lax.broadcasted_iota(jnp.int32, extra.shape, 1)
    named = []
    for e in range(per_group):
        mine = group * per_group + e
        pick = (lane == mine) | (lane == mine + experts)
        named.append(0.5 * jnp.sum(jnp.where(pick, extra, 0.0), axis=1, keepdims=True))

    per_expert = units // per_group
    nt = (((1,), (1,)), ((), ()))
    for h in range(2):
        gate, up = weights[3 * h], weights[3 * h + 1]
        for start, size in tiles(units):
            gate_pre = lax.dot_general(
                rows[:, :depth],
                gate[start : start + size],
                nt,
                preferred_element_type=jnp.float32,
            )
            up_pre = lax.dot_general(
                rows[:, :depth],
                up[start : start + size],
                nt,
                preferred_element_type=jnp.float32,
            )
            low, high = start // per_expert, (start + size - 1) // per_expert
            column = lax.broadcasted_iota(jnp.int32, (1, size), 1) + start
            scale = named[high]
            for e in range(high - 1, low - 1, -1):
                scale = jnp.where(column < (e + 1) * per_expert, named[e], scale)
            value = gate_pre * (1.0 + jnp.tanh(0.5 * gate_pre)) * (up_pre * scale)
            hidden[h, :, start : start + size] = value.astype(jnp.bfloat16)
    for start, size in tiles(depth):
        part = sum(
            jnp.dot(
                hidden[h],
                weights[3 * h + 2][:, start : start + size],
                preferred_element_type=jnp.float32,
            )
            for h in range(2)
        )
        to = slice(start % half, start % half + size)
        for jy in range(ny):
            for jx in range(nx):
                at = (jy * nx + jx) * tok
                block = part[at : at + tok]
                if start < half:
                    there = slice(jx * tok, (jx + 1) * tok)
                    if jy:
                        send_a[jy - 1, there, to] = block.astype(jnp.bfloat16)
                    else:
                        keep_a[there, to] = block
                else:
                    there = slice(jy * tok, (jy + 1) * tok)
                    if jx:
                        send_b[jx - 1, there, to] = block.astype(jnp.bfloat16)
                    else:
                        keep_b[there, to] = block


def ffn(first, near, left, right, weights, place, experts, per_group):
    ny, nx = len(left) + 1, len(right) + 1
    tok, width = first.shape
    units, depth = weights[0].shape
    half, count = depth // 2, ny * nx * tok
    any_spec, vmem = pl.BlockSpec(memory_space=pl.ANY), pl.BlockSpec(memory_space=pltpu.VMEM)
    sources = [first, *near, *left, *right]
    macs = count * depth * units * 6
    return pl.pallas_call(
        functools.partial(ffn_kernel, ny, nx, experts, per_group),
        in_specs=[pl.BlockSpec(memory_space=pltpu.SMEM)] + [any_spec] * len(sources) + [vmem] * 6,
        out_specs=[vmem] * 4,
        out_shape=[
            jax.ShapeDtypeStruct((ny - 1, nx * tok, half), jnp.bfloat16),
            jax.ShapeDtypeStruct((nx * tok, half), jnp.float32),
            jax.ShapeDtypeStruct((nx - 1, ny * tok, half), jnp.bfloat16),
            jax.ShapeDtypeStruct((ny * tok, half), jnp.float32),
        ],
        scratch_shapes=[
            pltpu.VMEM((count, width), jnp.bfloat16),
            pltpu.VMEM((2, count, units), jnp.bfloat16),
            pltpu.SemaphoreType.DMA((2 * ny * nx,)),
        ],
        compiler_params=pltpu.CompilerParams(vmem_limit_bytes=26 * 1024 * 1024),
        cost_estimate=pl.CostEstimate(
            flops=2 * macs,
            bytes_accessed=8 * count * depth,
            transcendentals=2 * count * units,
        ),
    )(place, *sources, *weights)


def shift(value, axis, by):
    n = lax.axis_size(axis)
    return lax.ppermute(value, axis, [(i, (i + by) % n) for i in range(n)])


def ring_step(value):
    n = lax.axis_size("line")
    order = list(range(1, n, 2)) + list(range(0, n, 2))[::-1]
    return lax.ppermute(value, "line", [(order[i], order[(i + 1) % n]) for i in range(n)])


def after(value, *earlier):
    return lax.optimization_barrier((value, earlier))[0]


def per_device(tokens, expert_ids, combine, gate_weight, up_weight, down_weight):
    ny, nx, stages = lax.axis_size("e_hi"), lax.axis_size("e_lo"), lax.axis_size("line")
    per_group, units, depth = gate_weight.shape
    experts = ny * nx * per_group
    tok = tokens.shape[0]
    half = depth // 2
    group = lax.axis_index(("e_hi", "e_lo")).astype(jnp.int32).reshape(1)

    chosen = expert_ids[:, :, None] == jnp.arange(experts, dtype=jnp.int32)[None, None, :]
    named = jnp.sum(jnp.where(chosen, combine[:, :, None], 0.0), axis=1)
    high = named.astype(jnp.bfloat16)
    rest = (named - high.astype(jnp.float32)).astype(jnp.bfloat16)
    pad = jnp.zeros((tok, LANES * -(-2 * experts // LANES) - 2 * experts), jnp.bfloat16)
    first = jnp.concatenate([tokens, high, rest, pad], axis=1)

    def near_of(pieces):
        if nx == ny:
            lefts, rights = pieces[: nx - 1], pieces[nx - 1 :]
            return [jnp.concatenate([a, b], axis=1) for a, b in zip(lefts, rights)]
        return pieces

    def halves_of(near):
        if nx == ny:
            return [n[:, :half] for n in near], [n[:, half:] for n in near]
        return near[: nx - 1], near[nx - 1 :]

    near = [shift(tokens[:, :half], "e_lo", j) for j in range(1, nx)]
    near += [shift(first[:, half:], "e_hi", j) for j in range(1, ny)]
    near = near_of(near)

    own = [w.reshape(per_group * units, depth) for w in (gate_weight, up_weight, down_weight)]
    other = [shift(own[0], "core", 1)]

    def add(*terms):
        return sum(t.astype(jnp.float32) for t in terms)

    def exchange(first, near):
        lefts, rights = halves_of(near)
        left = jnp.concatenate([first[:, :half], *lefts])
        right = jnp.concatenate([first[:, half:], *rights])
        return (
            [shift(left, "e_hi", j) for j in range(1, ny)],
            [shift(right, "e_lo", j) for j in range(1, nx)],
        )

    def run(first, near, sides, *earlier):
        first, sides = after((first, sides), *earlier)
        if nx == ny:
            lefts, rights = halves_of(near)
            near = lefts + rights
        return ffn(first, near, *sides, weights, group, experts, per_group)

    def start_sums(parts, *earlier):
        send_a, keep_a, send_b, keep_b = parts
        send_a, send_b = after((send_a, send_b), *earlier)
        got_a = [shift(send_a[j - 1], "e_hi", -j) for j in range(1, ny)]
        got_b = [shift(send_b[j - 1], "e_lo", -j) for j in range(1, nx)]
        return [keep_a] + got_a, [keep_b] + got_b

    def finish_sums(terms_a, terms_b):
        sum_a = add(*terms_a).reshape(nx, tok, half)
        sum_b = add(*terms_b).reshape(ny, tok, half)
        last_a = [shift(sum_a[j].astype(jnp.bfloat16), "e_lo", -j) for j in range(1, nx)]
        last_b = [shift(sum_b[j].astype(jnp.bfloat16), "e_hi", -j) for j in range(1, ny)]
        return [sum_a[0]] + last_a, [sum_b[0]] + last_b

    firsts, nears, sides = [first], [near], [exchange(first, near)]
    firsts.append(ring_step(first))
    nears.append([ring_step(n) for n in near])
    other.append(shift(after(own[1], other[0], near, firsts[1]), "core", 1))
    other.append(shift(after(own[2], other[0], near, firsts[1]), "core", 1))
    weights = own + other

    parts, begun = {}, {}
    for k in range(1, stages):
        sides.append(exchange(firsts[k], nears[k]))
        if k + 1 < stages:
            if nx == ny:
                pair = jnp.concatenate([firsts[k], *nears[k]])
                pair = ring_step(pair)
                firsts.append(pair[:tok])
                nears.append([pair[i * tok : (i + 1) * tok] for i in range(1, nx)])
            else:
                firsts.append(ring_step(firsts[k]))
                nears.append([ring_step(n) for n in nears[k]])
        earlier = firsts[k], nears[k], begun.get(k - 2)
        parts[k - 1] = run(firsts[k - 1], nears[k - 1], sides[k - 1], *earlier)
        begun[k - 1] = start_sums(parts[k - 1], sides[k])
    last = stages - 1
    parts[last] = run(firsts[last], nears[last], sides[last], parts[last - 1])
    begun[last] = start_sums(parts[last], begun[last - 1])

    carry_a, carry_b = [], []
    for k in list(range(1, stages)) + [0]:
        terms_a, terms_b = begun[k]
        if k == 1:
            sums = jnp.concatenate([add(*terms_a), add(*terms_b)], axis=1 if nx == ny else 0)
            sums = ring_step(sums.astype(jnp.bfloat16))
            if nx == ny:
                mid_a, mid_b = [sums[:, :half]], [sums[:, half:]]
            else:
                mid_a, mid_b = [sums[: nx * tok]], [sums[nx * tok :]]
            continue
        if k == 0:
            mid_a, mid_b = [], []
        a, b = finish_sums(terms_a + mid_a, terms_b + mid_b)
        mid_a, mid_b = [], []
        total = jnp.concatenate([add(*a, *carry_a), add(*b, *carry_b)], axis=1)
        total = total.astype(jnp.bfloat16)
        if k:
            total = ring_step(total)
            carry_a, carry_b = [total[:, :half]], [total[:, half:]]
    return total


def solution(mesh):
    groups, shards = mesh.shape["expert"], mesh.shape["fsdp"]
    split = Mesh(mesh.devices.reshape(groups // 2, 2, shards // 2, 2), AXES)
    whole, expert, shard = P(AXES, None), ("e_hi", "e_lo"), ("line", "core")
    return jax.shard_map(
        per_device,
        mesh=split,
        in_specs=(whole, whole, whole) + (P(expert, shard, None),) * 3,
        out_specs=whole,
        check_vma=False,
    )
```

profile of v0, /device:TPU:0, one launch (start us, length us, event | category | flops | bytes accessed | tf_op | source)
XLA Modules:
  0.0 189.5 jit_solution(11200763130174561128)
XLA Ops:
  0.5 1.0 slice.135
  1.4 2.6 %collective-permute-start = (bf16[144,1024]{1,0:T(8,128)(2,1)S(1)}, bf16[144,1024]{1,0:T(8,128)(2,1)S(1)}, u32[]{:S(2)}, u32[]{:S(2)}) collective-permute-start(bf16[144,1024]{1,0:T(8,128)(2,1)S(1)} %slice.135), channel_id=1, source_target_pairs={{0,8},{8,0},{1,9},{9,1},{2,10},{10,2},{3,11},{11,3},{4,12},{12,4},... | collective-permute-start | bytes 884744 | tf_op jit(solution)/shard_map/ppermute | solution.py:156
  4.1 0.7 select_reduce_fusion
  5.4 1.6 collective-permute-start.4
  7.0 1.6 collective-permute-start.2
  8.6 3.1 %collective-permute-done.refs_2_ = bf16[144,1024]{1,0:T(8,128)(2,1)S(1)} collective-permute-done((bf16[144,1024]{1,0:T(8,128)(2,1)S(1)}, bf16[144,1024]{1,0:T(8,128)(2,1)S(1)}, u32[]{:S(2)}, u32[]{:S(2)}) %collective-permute-start) | collective-permute-done | bytes 294944 | tf_op jit(solution)/shard_map/ppermute | solution.py:156
  11.7 0.8 constant_dynamic-update-slice_fusion.1
  12.4 4.2 %collective-permute-done.2.refs_3_ = bf16[144,1152]{1,0:T(8,128)(2,1)S(1)} collective-permute-done((bf16[144,1152]{1,0:T(8,128)(2,1)S(1)}, bf16[144,1152]{1,0:T(8,128)(2,1)S(1)}, u32[]{:S(2)}, u32[]{:S(2)}) %collective-permute-start.2) | collective-permute-done | bytes 331808 | tf_op jit(solution)/shard_map/ppermute | solution.py:156
  16.7 0.8 constant_dynamic-update-slice_fusion
  17.4 5.1 %collective-permute-done.4.refs_1_ = bf16[144,2176]{1,0:T(8,128)(2,1)S(1)} collective-permute-done((bf16[144,2176]{1,0:T(8,128)(2,1)S(1)}, bf16[144,2176]{1,0:T(8,128)(2,1)S(1)}, u32[]{:S(2)}, u32[]{:S(2)}) %collective-permute-start.4) | collective-permute-done | bytes 626720 | tf_op jit(solution)/shard_map/ppermute | solution.py:162
  23.0 0.8 collective-permute-start.5
  23.8 1.6 collective-permute-start.1
  25.5 0.6 collective-permute-start.3
  26.1 14.1 %collective-permute-done.5 = bf16[144,2176]{1,0:T(8,128)(2,1)S(1)} collective-permute-done((bf16[144,2176]{1,0:T(8,128)(2,1)}, bf16[144,2176]{1,0:T(8,128)(2,1)S(1)}, u32[]{:S(2)}, u32[]{:S(2)}) %collective-permute-start.5) | collective-permute-done | bytes 626720 | tf_op jit(solution)/shard_map/ppermute | solution.py:162
  40.3 1.6 collective-permute-start.9
  42.1 0.6 collective-permute-start.10
  42.7 3.1 %collective-permute-start.13 = (bf16[288,2176]{1,0:T(8,128)(2,1)S(1)}, bf16[288,2176]{1,0:T(8,128)(2,1)S(1)}, u32[]{:S(2)}, u32[]{:S(2)}) collective-permute-start(bf16[288,2176]{1,0:T(8,128)(2,1)S(1)} %pad_maximum_fusion), channel_id=1, source_target_pairs={{2,6},{6,4},{4,0},{0,2},{3,7},{7,5},{5,1},{1,3},{10,14},{14,12},{1... | collective-permute-start | bytes 3760136 | tf_op jit(solution)/shard_map/ppermute | solution.py:162
  45.9 15.0 %shard_map.64 = (bf16[1,288,1024]{2,1,0:T(8,128)(2,1)S(1)}, f32[288,1024]{1,0:T(8,128)S(1)}, bf16[1,288,1024]{2,1,0:T(8,128)(2,1)S(1)}, f32[288,1024]{1,0:T(8,128)S(1)}) custom-call(s32[1]{0:T(128)} %bitcast.refs_0_, bf16[144,2176]{1,0:T(8,128)(2,1)S(1)} %concatenate.50.refs_1_, bf16[144,1024]{1,0:T(8,128)(2,1)S(1)} %collective-permute-done.refs_2_, ...), custom_call_target="tpu_custom_call" | custom-call | flops 9965666304 | bytes 9437184 | tf_op jit(solution)/shard_map/pallas_call | solution.py:130
  61.5 10.2 %collective-permute-done.13 = bf16[288,2176]{1,0:T(8,128)(2,1)S(1)} collective-permute-done((bf16[288,2176]{1,0:T(8,128)(2,1)S(1)}, bf16[288,2176]{1,0:T(8,128)(2,1)S(1)}, u32[]{:S(2)}, u32[]{:S(2)}) %collective-permute-start.13) | collective-permute-done | bytes 1253408 | tf_op jit(solution)/shard_map/ppermute | solution.py:162
  71.8 1.2 collective-permute-start.17
  73.1 1.6 collective-permute-start.18
  74.7 1.0 collective-permute-start.14
  76.1 15.0 %shard_map.65 = (bf16[1,288,1024]{2,1,0:T(8,128)(2,1)S(1)}, f32[288,1024]{1,0:T(8,128)S(1)}, bf16[1,288,1024]{2,1,0:T(8,128)(2,1)S(1)}, f32[288,1024]{1,0:T(8,128)S(1)}) custom-call(s32[1]{0:T(128)} %bitcast.refs_0_, bf16[144,2176]{1,0:T(8,128)(2,1)S(1)} %copy-done.1, bf16[144,1024]{1,0:T(8,128)(2,1)S(1)} %slice.167.refs_2_, ...), custom_call_target="tpu_custom_call" | custom-call | flops 9965666304 | bytes 9437184 | tf_op jit(solution)/shard_map/pallas_call | solution.py:130
  91.2 1.6 collective-permute-start.21
  93.1 9.7 %collective-permute-done.14 = bf16[288,2176]{1,0:T(8,128)(2,1)S(1)} collective-permute-done((bf16[288,2176]{1,0:T(8,128)(2,1)S(1)}, bf16[288,2176]{1,0:T(8,128)(2,1)S(1)}, u32[]{:S(2)}, u32[]{:S(2)}) %collective-permute-start.14) | collective-permute-done | bytes 1253408 | tf_op jit(solution)/shard_map/ppermute | solution.py:162
  102.8 0.7 collective-permute-start.15
  103.5 0.6 collective-permute-start.16
  104.3 0.7 collective-permute-done.20
  105.4 6.2 %collective-permute-start.26 = (bf16[288,2048]{1,0:T(8,128)(2,1)S(1)}, bf16[288,2048]{1,0:T(8,128)(2,1)S(1)}, u32[]{:S(2)}, u32[]{:S(2)}) collective-permute-start(bf16[288,2048]{1,0:T(8,128)(2,1)S(1)} %pad_maximum_fusion.1), channel_id=1, source_target_pairs={{2,6},{6,4},{4,0},{0,2},{3,7},{7,5},{5,1},{1,3},{10,14},{14,12},{1... | collective-permute-start | bytes 3538952 | tf_op jit(solution)/shard_map/ppermute | solution.py:162
  111.7 15.0 %shard_map.66 = (bf16[1,288,1024]{2,1,0:T(8,128)(2,1)S(1)}, f32[288,1024]{1,0:T(8,128)S(1)}, bf16[1,288,1024]{2,1,0:T(8,128)(2,1)S(1)}, f32[288,1024]{1,0:T(8,128)S(1)}) custom-call(s32[1]{0:T(128)} %bitcast.refs_0_, bf16[144,2176]{1,0:T(8,128)(2,1)S(1)} %slice.173.refs_1_, bf16[144,1024]{1,0:T(8,128)(2,1)S(1)} %slice.174.refs_2_, ...), custom_call_target="tpu_custom_call" | custom-call | flops 9965666304 | bytes 9437184 | tf_op jit(solution)/shard_map/pallas_call | solution.py:130
  126.8 2.4 %collective-permute-start.23 = (bf16[288,1024]{1,0:T(8,128)(2,1)S(1)}, bf16[288,1024]{1,0:T(8,128)(2,1)S(1)}, u32[]{:S(2)}, u32[]{:S(2)}) collective-permute-start(bf16[288,1024]{1,0:T(8,128)(2,1)S(1)} %bitcast.34), channel_id=1, source_target_pairs={{0,8},{8,0},{1,9},{9,1},{2,10},{10,2},{3,11},{11,3},{4,12},{12,4},... | collective-permute-start | bytes 1769480 | tf_op jit(solution)/shard_map/ppermute | solution.py:156
  129.1 0.9 collective-permute-start.22
  130.0 15.3 %shard_map.67 = (bf16[1,288,1024]{2,1,0:T(8,128)(2,1)S(1)}, f32[288,1024]{1,0:T(8,128)S(1)}, bf16[1,288,1024]{2,1,0:T(8,128)(2,1)S(1)}, f32[288,1024]{1,0:T(8,128)S(1)}) custom-call(s32[1]{0:T(128)} %bitcast.refs_0_, bf16[144,2176]{1,0:T(8,128)(2,1)S(1)} %slice.172.refs_1_, bf16[144,1024]{1,0:T(8,128)(2,1)S(1)} %slice.176.refs_2_, ...), custom_call_target="tpu_custom_call" | custom-call | flops 9965666304 | bytes 9437184 | tf_op jit(solution)/shard_map/pallas_call | solution.py:130
  145.5 1.1 collective-permute-start.24
  147.3 0.9 collective-permute-start.28
  148.2 1.9 %collective-permute-start.27 = (bf16[144,1024]{1,0:T(8,128)(2,1)S(1)}, bf16[144,1024]{1,0:T(8,128)(2,1)S(1)}, u32[]{:S(2)}, u32[]{:S(2)}) collective-permute-start(bf16[144,1024]{1,0:T(8,128)(2,1)S(1)} %slice.235), channel_id=1, source_target_pairs={{0,8},{8,0},{1,9},{9,1},{2,10},{10,2},{3,11},{11,3},{4,12},{12,4},... | collective-permute-start | bytes 884744 | tf_op jit(solution)/shard_map/ppermute | solution.py:156
  150.2 6.2 %collective-permute-done.30 = bf16[288,1024]{1,0:T(8,128)(2,1)S(1)} collective-permute-done((bf16[288,1024]{1,0:T(8,128)(2,1)S(1)}, bf16[288,1024]{1,0:T(8,128)(2,1)S(1)}, u32[]{:S(2)}, u32[]{:S(2)}) %collective-permute-start.30) | collective-permute-done | bytes 589856 | tf_op jit(solution)/shard_map/ppermute | solution.py:156
  156.6 2.8 %collective-permute-start.31 = (bf16[144,1024]{1,0:T(8,128)(2,1)S(1)}, bf16[144,1024]{1,0:T(8,128)(2,1)S(1)}, u32[]{:S(2)}, u32[]{:S(2)}) collective-permute-start(bf16[144,1024]{1,0:T(8,128)(2,1)S(1)} %slice.233), channel_id=1, source_target_pairs={{0,16},{16,0},{1,17},{17,1},{2,18},{18,2},{3,19},{19,3},{4,20},{20... | collective-permute-start | bytes 884744 | tf_op jit(solution)/shard_map/ppermute | solution.py:156
  159.4 1.7 collective-permute-done.28
  161.2 1.5 collective-permute-done.27
  163.2 1.6 collective-permute-start.25
  165.0 0.6 collective-permute-start.12
  165.6 4.4 %collective-permute-done.25 = bf16[144,1024]{1,0:T(8,128)(2,1)S(1)} collective-permute-done((bf16[144,1024]{1,0:T(8,128)(2,1)S(1)}, bf16[144,1024]{1,0:T(8,128)(2,1)S(1)}, u32[]{:S(2)}, u32[]{:S(2)}) %collective-permute-start.25) | collective-permute-done | bytes 294944 | tf_op jit(solution)/shard_map/ppermute | solution.py:156
  170.0 7.1 %collective-permute-done.29 = bf16[144,2048]{1,0:T(8,128)(2,1)S(1)} collective-permute-done((bf16[144,2048]{1,0:T(8,128)(2,1)S(1)}, bf16[144,2048]{1,0:T(8,128)(2,1)S(1)}, u32[]{:S(2)}, u32[]{:S(2)}) %collective-permute-start.29) | collective-permute-done | bytes 589856 | tf_op jit(solution)/shard_map/ppermute | solution.py:162
  177.5 1.1 collective-permute-start.32
  178.9 6.7 %collective-permute-done.33 = bf16[144,1024]{1,0:T(8,128)(2,1)S(1)} collective-permute-done((bf16[144,1024]{1,0:T(8,128)(2,1)S(1)}, bf16[144,1024]{1,0:T(8,128)(2,1)S(1)}, u32[]{:S(2)}, u32[]{:S(2)}) %collective-permute-start.33) | collective-permute-done | bytes 294944 | tf_op jit(solution)/shard_map/ppermute | solution.py:156
  185.6 2.7 %collective-permute-done.32 = bf16[144,2048]{1,0:T(8,128)(2,1)S(1)} collective-permute-done((bf16[144,2048]{1,0:T(8,128)(2,1)S(1)}, bf16[144,2048]{1,0:T(8,128)(2,1)S(1)}, u32[]{:S(2)}, u32[]{:S(2)}) %collective-permute-start.32) | collective-permute-done | bytes 589856 | tf_op jit(solution)/shard_map/ppermute | solution.py:162
  188.6 0.9 pad_maximum_fusion.8
  (88 shorter events, 6.8 us)
Async XLA Ops:
  0.0 5.1 %copy-start.5 = (bf16[144,2048]{1,0:T(8,128)(2,1)S(1)}, bf16[144,2048]{1,0:T(8,128)(2,1)}, u32[]{:S(2)}) copy-start(bf16[144,2048]{1,0:T(8,128)(2,1)} %param.6) | copy-start | bytes 1769476
  0.0 22.5 %collective-permute-start.6 = (bf16[704,2048]{1,0:T(8,128)(2,1)}, bf16[704,2048]{1,0:T(8,128)(2,1)}, u32[]{:S(2)}, u32[]{:S(2)}) collective-permute-start(bf16[704,2048]{1,0:T(8,128)(2,1)} %bitcast.12), channel_id=1, source_target_pairs={{0,1},{1,0},{2,3},{3,2},{4,5},{5,4},{6,7},{7,6},{8,9},{9,8},{10,11... | collective-permute-start | bytes 8650760 | tf_op jit(solution)/shard_map/ppermute | solution.py:156
  1.4 10.2 %collective-permute-start = (bf16[144,1024]{1,0:T(8,128)(2,1)S(1)}, bf16[144,1024]{1,0:T(8,128)(2,1)S(1)}, u32[]{:S(2)}, u32[]{:S(2)}) collective-permute-start(bf16[144,1024]{1,0:T(8,128)(2,1)S(1)} %slice.135), channel_id=1, source_target_pairs={{0,8},{8,0},{1,9},{9,1},{2,10},{10,2},{3,11},{11,3},{4,12},{12,4},... | collective-permute-start | bytes 884744 | tf_op jit(solution)/shard_map/ppermute | solution.py:156
  5.4 17.1 %collective-permute-start.4 = (bf16[144,2176]{1,0:T(8,128)(2,1)S(1)}, bf16[144,2176]{1,0:T(8,128)(2,1)S(1)}, u32[]{:S(2)}, u32[]{:S(2)}) collective-permute-start(bf16[144,2176]{1,0:T(8,128)(2,1)S(1)} %concatenate.50.refs_1_), channel_id=1, source_target_pairs={{2,6},{6,4},{4,0},{0,2},{3,7},{7,5},{5,1},{1,3},{10,14},{14,12},{1... | collective-permute-start | bytes 1880072 | tf_op jit(solution)/shard_map/ppermute | solution.py:162
  7.0 9.6 %collective-permute-start.2 = (bf16[144,1152]{1,0:T(8,128)(2,1)S(1)}, bf16[144,1152]{1,0:T(8,128)(2,1)S(1)}, u32[]{:S(2)}, u32[]{:S(2)}) collective-permute-start(bf16[144,1152]{1,0:T(8,128)(2,1)S(1)} %slice.165), channel_id=1, source_target_pairs={{0,16},{16,0},{1,17},{17,1},{2,18},{18,2},{3,19},{19,3},{4,20},{20... | collective-permute-start | bytes 995336 | tf_op jit(solution)/shard_map/ppermute | solution.py:156
  22.5 3.6 %copy-start = (bf16[144,2176]{1,0:T(8,128)(2,1)}, bf16[144,2176]{1,0:T(8,128)(2,1)S(1)}, u32[]{:S(2)}) copy-start(bf16[144,2176]{1,0:T(8,128)(2,1)S(1)} %collective-permute-done.4.refs_1_) | copy-start | bytes 1880068
  22.5 23.3 %collective-permute-start.7 = (bf16[704,2048]{1,0:T(8,128)(2,1)}, bf16[704,2048]{1,0:T(8,128)(2,1)}, u32[]{:S(2)}, u32[]{:S(2)}) collective-permute-start(bf16[704,2048]{1,0:T(8,128)(2,1)} %bitcast.17), channel_id=1, source_target_pairs={{0,1},{1,0},{2,3},{3,2},{4,5},{5,4},{6,7},{7,6},{8,9},{9,8},{10,11... | collective-permute-start | bytes 8650760 | tf_op jit(solution)/shard_map/ppermute | solution.py:156
  22.5 23.3 %collective-permute-start.8 = (bf16[704,2048]{1,0:T(8,128)(2,1)}, bf16[704,2048]{1,0:T(8,128)(2,1)}, u32[]{:S(2)}, u32[]{:S(2)}) collective-permute-start(bf16[704,2048]{1,0:T(8,128)(2,1)} %bitcast.22), channel_id=1, source_target_pairs={{0,1},{1,0},{2,3},{3,2},{4,5},{5,4},{6,7},{7,6},{8,9},{9,8},{10,11... | collective-permute-start | bytes 8650760 | tf_op jit(solution)/shard_map/ppermute | solution.py:156
  23.0 17.2 %collective-permute-start.5 = (bf16[144,2176]{1,0:T(8,128)(2,1)}, bf16[144,2176]{1,0:T(8,128)(2,1)S(1)}, u32[]{:S(2)}, u32[]{:S(2)}) collective-permute-start(bf16[144,2176]{1,0:T(8,128)(2,1)} %constant_dynamic-update-slice_fusion), channel_id=1, source_target_pairs={{2,6},{6,4},{4,0},{0,2},{3,7},{7,5},{5,1},{1,3},{10,14},{14,12},{1... | collective-permute-start | bytes 1880072 | tf_op jit(solution)/shard_map/ppermute | solution.py:162
  23.8 22.0 %copy-start.4 = (bf16[4,176,2048]{2,1,0:T(8,128)(2,1)S(1)}, bf16[4,176,2048]{2,1,0:T(8,128)(2,1)}, u32[]{:S(2)}) copy-start(bf16[4,176,2048]{2,1,0:T(8,128)(2,1)} %param.11) | copy-start | bytes 8650756
  23.8 18.3 %collective-permute-start.1 = (bf16[288,1024]{1,0:T(8,128)(2,1)S(1)}, bf16[288,1024]{1,0:T(8,128)(2,1)S(1)}, u32[]{:S(2)}, u32[]{:S(2)}) collective-permute-start(bf16[288,1024]{1,0:T(8,128)(2,1)S(1)} %pad_maximum_fusion.4), channel_id=1, source_target_pairs={{0,16},{16,0},{1,17},{17,1},{2,18},{18,2},{3,19},{19,3},{4,20},{20... | collective-permute-start | bytes 1769480 | tf_op jit(solution)/shard_map/ppermute | solution.py:156
  25.5 17.2 %collective-permute-start.3 = (bf16[288,1152]{1,0:T(8,128)(2,1)S(1)}, bf16[288,1152]{1,0:T(8,128)(2,1)S(1)}, u32[]{:S(2)}, u32[]{:S(2)}) collective-permute-start(bf16[288,1152]{1,0:T(8,128)(2,1)S(1)} %pad_maximum_fusion.2), channel_id=1, source_target_pairs={{0,8},{8,0},{1,9},{9,1},{2,10},{10,2},{3,11},{11,3},{4,12},{12,4},... | collective-permute-start | bytes 1990664 | tf_op jit(solution)/shard_map/ppermute | solution.py:156
  26.1 19.7 %copy-start.3 = (bf16[4,176,2048]{2,1,0:T(8,128)(2,1)S(1)}, bf16[4,176,2048]{2,1,0:T(8,128)(2,1)}, u32[]{:S(2)}) copy-start(bf16[4,176,2048]{2,1,0:T(8,128)(2,1)} %param.10) | copy-start | bytes 8650756
  26.1 15.8 %slice-start = ((bf16[144,2176]{1,0:T(8,128)(2,1)}), bf16[144,1152]{1,0:T(8,128)(2,1)S(1)}, s32[]{:S(2)}) async-start(bf16[144,2176]{1,0:T(8,128)(2,1)} %copy-done), calls=%async_computation | async-start | bytes 663552 | tf_op jit(solution)/shard_map/slice | solution.py:208
  40.3 1.7 copy-start.1
  40.3 20.6 %collective-permute-start.9 = (bf16[288,1024]{1,0:T(8,128)(2,1)S(1)}, bf16[288,1024]{1,0:T(8,128)(2,1)S(1)}, u32[]{:S(2)}, u32[]{:S(2)}) collective-permute-start(bf16[288,1024]{1,0:T(8,128)(2,1)S(1)} %pad_maximum_fusion.5), channel_id=1, source_target_pairs={{0,16},{16,0},{1,17},{17,1},{2,18},{18,2},{3,19},{19,3},{4,20},{20... | collective-permute-start | bytes 1769480 | tf_op jit(solution)/shard_map/ppermute | solution.py:156
  41.9 3.9 %copy-start.2 = (bf16[4,176,2048]{2,1,0:T(8,128)(2,1)S(1)}, bf16[4,176,2048]{2,1,0:T(8,128)(2,1)}, u32[]{:S(2)}) copy-start(bf16[4,176,2048]{2,1,0:T(8,128)(2,1)} %param.9) | copy-start | bytes 8650756
  42.1 18.8 %collective-permute-start.10 = (bf16[288,1152]{1,0:T(8,128)(2,1)S(1)}, bf16[288,1152]{1,0:T(8,128)(2,1)S(1)}, u32[]{:S(2)}, u32[]{:S(2)}) collective-permute-start(bf16[288,1152]{1,0:T(8,128)(2,1)S(1)} %pad_maximum_fusion.3), channel_id=1, source_target_pairs={{0,8},{8,0},{1,9},{9,1},{2,10},{10,2},{3,11},{11,3},{4,12},{12,4},... | collective-permute-start | bytes 1990664 | tf_op jit(solution)/shard_map/ppermute | solution.py:156
  42.7 29.0 %collective-permute-start.13 = (bf16[288,2176]{1,0:T(8,128)(2,1)S(1)}, bf16[288,2176]{1,0:T(8,128)(2,1)S(1)}, u32[]{:S(2)}, u32[]{:S(2)}) collective-permute-start(bf16[288,2176]{1,0:T(8,128)(2,1)S(1)} %pad_maximum_fusion), channel_id=1, source_target_pairs={{2,6},{6,4},{4,0},{0,2},{3,7},{7,5},{5,1},{1,3},{10,14},{14,12},{1... | collective-permute-start | bytes 3760136 | tf_op jit(solution)/shard_map/ppermute | solution.py:162
  60.9 14.8 %collective-permute-start.19 = (bf16[288,1024]{1,0:T(8,128)(2,1)S(1)}, bf16[288,1024]{1,0:T(8,128)(2,1)S(1)}, u32[]{:S(2)}, u32[]{:S(2)}) collective-permute-start(bf16[288,1024]{1,0:T(8,128)(2,1)S(1)} %bitcast.32), channel_id=1, source_target_pairs={{0,8},{8,0},{1,9},{9,1},{2,10},{10,2},{3,11},{11,3},{4,12},{12,4},... | collective-permute-start | bytes 1769480 | tf_op jit(solution)/shard_map/ppermute | solution.py:156
  61.5 14.6 %collective-permute-start.11 = (bf16[288,1024]{1,0:T(8,128)(2,1)S(1)}, bf16[288,1024]{1,0:T(8,128)(2,1)S(1)}, u32[]{:S(2)}, u32[]{:S(2)}) collective-permute-start(bf16[288,1024]{1,0:T(8,128)(2,1)S(1)} %bitcast.30), channel_id=1, source_target_pairs={{0,16},{16,0},{1,17},{17,1},{2,18},{18,2},{3,19},{19,3},{4,20},{20... | collective-permute-start | bytes 1769480 | tf_op jit(solution)/shard_map/ppermute | solution.py:156
  71.8 19.4 %collective-permute-start.17 = (bf16[288,1024]{1,0:T(8,128)(2,1)S(1)}, bf16[288,1024]{1,0:T(8,128)(2,1)S(1)}, u32[]{:S(2)}, u32[]{:S(2)}) collective-permute-start(bf16[288,1024]{1,0:T(8,128)(2,1)S(1)} %concatenate.67), channel_id=1, source_target_pairs={{0,16},{16,0},{1,17},{17,1},{2,18},{18,2},{3,19},{19,3},{4,20},{20... | collective-permute-start | bytes 1769480 | tf_op jit(solution)/shard_map/ppermute | solution.py:156
  73.1 18.1 %collective-permute-start.18 = (bf16[288,1152]{1,0:T(8,128)(2,1)S(1)}, bf16[288,1152]{1,0:T(8,128)(2,1)S(1)}, u32[]{:S(2)}, u32[]{:S(2)}) collective-permute-start(bf16[288,1152]{1,0:T(8,128)(2,1)S(1)} %concatenate.68), channel_id=1, source_target_pairs={{0,8},{8,0},{1,9},{9,1},{2,10},{10,2},{3,11},{11,3},{4,12},{12,4},... | collective-permute-start | bytes 1990664 | tf_op jit(solution)/shard_map/ppermute | solution.py:156
  74.7 28.1 %collective-permute-start.14 = (bf16[288,2176]{1,0:T(8,128)(2,1)S(1)}, bf16[288,2176]{1,0:T(8,128)(2,1)S(1)}, u32[]{:S(2)}, u32[]{:S(2)}) collective-permute-start(bf16[288,2176]{1,0:T(8,128)(2,1)S(1)} %collective-permute-done.13), channel_id=1, source_target_pairs={{2,6},{6,4},{4,0},{0,2},{3,7},{7,5},{5,1},{1,3},{10,14},{14,12},{1... | collective-permute-start | bytes 3760136 | tf_op jit(solution)/shard_map/ppermute | solution.py:162
  91.2 13.1 %collective-permute-start.21 = (bf16[288,1024]{1,0:T(8,128)(2,1)S(1)}, bf16[288,1024]{1,0:T(8,128)(2,1)S(1)}, u32[]{:S(2)}, u32[]{:S(2)}) collective-permute-start(bf16[288,1024]{1,0:T(8,128)(2,1)S(1)} %bitcast.31), channel_id=1, source_target_pairs={{0,8},{8,0},{1,9},{9,1},{2,10},{10,2},{3,11},{11,3},{4,12},{12,4},... | collective-permute-start | bytes 1769480 | tf_op jit(solution)/shard_map/ppermute | solution.py:156
  92.8 12.2 %collective-permute-start.20 = (bf16[288,1024]{1,0:T(8,128)(2,1)S(1)}, bf16[288,1024]{1,0:T(8,128)(2,1)S(1)}, u32[]{:S(2)}, u32[]{:S(2)}) collective-permute-start(bf16[288,1024]{1,0:T(8,128)(2,1)S(1)} %bitcast.29), channel_id=1, source_target_pairs={{0,16},{16,0},{1,17},{17,1},{2,18},{18,2},{3,19},{19,3},{4,20},{20... | collective-permute-start | bytes 1769480 | tf_op jit(solution)/shard_map/ppermute | solution.py:156
  102.8 23.9 %collective-permute-start.15 = (bf16[288,1024]{1,0:T(8,128)(2,1)S(1)}, bf16[288,1024]{1,0:T(8,128)(2,1)S(1)}, u32[]{:S(2)}, u32[]{:S(2)}) collective-permute-start(bf16[288,1024]{1,0:T(8,128)(2,1)S(1)} %concatenate.65), channel_id=1, source_target_pairs={{0,16},{16,0},{1,17},{17,1},{2,18},{18,2},{3,19},{19,3},{4,20},{20... | collective-permute-start | bytes 1769480 | tf_op jit(solution)/shard_map/ppermute | solution.py:156
  103.5 23.2 %collective-permute-start.16 = (bf16[288,1152]{1,0:T(8,128)(2,1)S(1)}, bf16[288,1152]{1,0:T(8,128)(2,1)S(1)}, u32[]{:S(2)}, u32[]{:S(2)}) collective-permute-start(bf16[288,1152]{1,0:T(8,128)(2,1)S(1)} %concatenate.66), channel_id=1, source_target_pairs={{0,8},{8,0},{1,9},{9,1},{2,10},{10,2},{3,11},{11,3},{4,12},{12,4},... | collective-permute-start | bytes 1990664 | tf_op jit(solution)/shard_map/ppermute | solution.py:156
  105.4 41.2 %collective-permute-start.26 = (bf16[288,2048]{1,0:T(8,128)(2,1)S(1)}, bf16[288,2048]{1,0:T(8,128)(2,1)S(1)}, u32[]{:S(2)}, u32[]{:S(2)}) collective-permute-start(bf16[288,2048]{1,0:T(8,128)(2,1)S(1)} %pad_maximum_fusion.1), channel_id=1, source_target_pairs={{2,6},{6,4},{4,0},{0,2},{3,7},{7,5},{5,1},{1,3},{10,14},{14,12},{1... | collective-permute-start | bytes 3538952 | tf_op jit(solution)/shard_map/ppermute | solution.py:162
  126.8 18.5 %collective-permute-start.23 = (bf16[288,1024]{1,0:T(8,128)(2,1)S(1)}, bf16[288,1024]{1,0:T(8,128)(2,1)S(1)}, u32[]{:S(2)}, u32[]{:S(2)}) collective-permute-start(bf16[288,1024]{1,0:T(8,128)(2,1)S(1)} %bitcast.34), channel_id=1, source_target_pairs={{0,8},{8,0},{1,9},{9,1},{2,10},{10,2},{3,11},{11,3},{4,12},{12,4},... | collective-permute-start | bytes 1769480 | tf_op jit(solution)/shard_map/ppermute | solution.py:156
  129.1 16.2 %collective-permute-start.22 = (bf16[288,1024]{1,0:T(8,128)(2,1)S(1)}, bf16[288,1024]{1,0:T(8,128)(2,1)S(1)}, u32[]{:S(2)}, u32[]{:S(2)}) collective-permute-start(bf16[288,1024]{1,0:T(8,128)(2,1)S(1)} %bitcast.33), channel_id=1, source_target_pairs={{0,16},{16,0},{1,17},{17,1},{2,18},{18,2},{3,19},{19,3},{4,20},{20... | collective-permute-start | bytes 1769480 | tf_op jit(solution)/shard_map/ppermute | solution.py:156
  145.3 11.0 %collective-permute-start.30 = (bf16[288,1024]{1,0:T(8,128)(2,1)S(1)}, bf16[288,1024]{1,0:T(8,128)(2,1)S(1)}, u32[]{:S(2)}, u32[]{:S(2)}) collective-permute-start(bf16[288,1024]{1,0:T(8,128)(2,1)S(1)} %bitcast.28), channel_id=1, source_target_pairs={{0,8},{8,0},{1,9},{9,1},{2,10},{10,2},{3,11},{11,3},{4,12},{12,4},... | collective-permute-start | bytes 1769480 | tf_op jit(solution)/shard_map/ppermute | solution.py:156
  145.5 17.5 %collective-permute-start.24 = (bf16[288,1024]{1,0:T(8,128)(2,1)S(1)}, bf16[288,1024]{1,0:T(8,128)(2,1)S(1)}, u32[]{:S(2)}, u32[]{:S(2)}) collective-permute-start(bf16[288,1024]{1,0:T(8,128)(2,1)S(1)} %bitcast.27), channel_id=1, source_target_pairs={{0,16},{16,0},{1,17},{17,1},{2,18},{18,2},{3,19},{19,3},{4,20},{20... | collective-permute-start | bytes 1769480 | tf_op jit(solution)/shard_map/ppermute | solution.py:156
  147.3 13.8 %collective-permute-start.28 = (bf16[144,1024]{1,0:T(8,128)(2,1)S(1)}, bf16[144,1024]{1,0:T(8,128)(2,1)S(1)}, u32[]{:S(2)}, u32[]{:S(2)}) collective-permute-start(bf16[144,1024]{1,0:T(8,128)(2,1)S(1)} %slice.234), channel_id=1, source_target_pairs={{0,16},{16,0},{1,17},{17,1},{2,18},{18,2},{3,19},{19,3},{4,20},{20... | collective-permute-start | bytes 884744 | tf_op jit(solution)/shard_map/ppermute | solution.py:156
  148.2 14.4 %collective-permute-start.27 = (bf16[144,1024]{1,0:T(8,128)(2,1)S(1)}, bf16[144,1024]{1,0:T(8,128)(2,1)S(1)}, u32[]{:S(2)}, u32[]{:S(2)}) collective-permute-start(bf16[144,1024]{1,0:T(8,128)(2,1)S(1)} %slice.235), channel_id=1, source_target_pairs={{0,8},{8,0},{1,9},{9,1},{2,10},{10,2},{3,11},{11,3},{4,12},{12,4},... | collective-permute-start | bytes 884744 | tf_op jit(solution)/shard_map/ppermute | solution.py:156
  156.6 9.0 %collective-permute-start.31 = (bf16[144,1024]{1,0:T(8,128)(2,1)S(1)}, bf16[144,1024]{1,0:T(8,128)(2,1)S(1)}, u32[]{:S(2)}, u32[]{:S(2)}) collective-permute-start(bf16[144,1024]{1,0:T(8,128)(2,1)S(1)} %slice.233), channel_id=1, source_target_pairs={{0,16},{16,0},{1,17},{17,1},{2,18},{18,2},{3,19},{19,3},{4,20},{20... | collective-permute-start | bytes 884744 | tf_op jit(solution)/shard_map/ppermute | solution.py:156
  162.8 14.3 %collective-permute-start.29 = (bf16[144,2048]{1,0:T(8,128)(2,1)S(1)}, bf16[144,2048]{1,0:T(8,128)(2,1)S(1)}, u32[]{:S(2)}, u32[]{:S(2)}) collective-permute-start(bf16[144,2048]{1,0:T(8,128)(2,1)S(1)} %pad_maximum_fusion.6), channel_id=1, source_target_pairs={{2,6},{6,4},{4,0},{0,2},{3,7},{7,5},{5,1},{1,3},{10,14},{14,12},{1... | collective-permute-start | bytes 1769480 | tf_op jit(solution)/shard_map/ppermute | solution.py:162
  163.2 6.8 %collective-permute-start.25 = (bf16[144,1024]{1,0:T(8,128)(2,1)S(1)}, bf16[144,1024]{1,0:T(8,128)(2,1)S(1)}, u32[]{:S(2)}, u32[]{:S(2)}) collective-permute-start(bf16[144,1024]{1,0:T(8,128)(2,1)S(1)} %slice.236), channel_id=1, source_target_pairs={{0,8},{8,0},{1,9},{9,1},{2,10},{10,2},{3,11},{11,3},{4,12},{12,4},... | collective-permute-start | bytes 884744 | tf_op jit(solution)/shard_map/ppermute | solution.py:156
  165.0 13.9 %collective-permute-start.12 = (bf16[144,1024]{1,0:T(8,128)(2,1)S(1)}, bf16[144,1024]{1,0:T(8,128)(2,1)S(1)}, u32[]{:S(2)}, u32[]{:S(2)}) collective-permute-start(bf16[144,1024]{1,0:T(8,128)(2,1)S(1)} %slice.237), channel_id=1, source_target_pairs={{0,8},{8,0},{1,9},{9,1},{2,10},{10,2},{3,11},{11,3},{4,12},{12,4},... | collective-permute-start | bytes 884744 | tf_op jit(solution)/shard_map/ppermute | solution.py:156
  177.5 10.8 %collective-permute-start.32 = (bf16[144,2048]{1,0:T(8,128)(2,1)S(1)}, bf16[144,2048]{1,0:T(8,128)(2,1)S(1)}, u32[]{:S(2)}, u32[]{:S(2)}) collective-permute-start(bf16[144,2048]{1,0:T(8,128)(2,1)S(1)} %pad_maximum_fusion.7), channel_id=1, source_target_pairs={{2,6},{6,4},{4,0},{0,2},{3,7},{7,5},{5,1},{1,3},{10,14},{14,12},{1... | collective-permute-start | bytes 1769480 | tf_op jit(solution)/shard_map/ppermute | solution.py:162
  178.8 6.8 %collective-permute-start.33 = (bf16[144,1024]{1,0:T(8,128)(2,1)S(1)}, bf16[144,1024]{1,0:T(8,128)(2,1)S(1)}, u32[]{:S(2)}, u32[]{:S(2)}) collective-permute-start(bf16[144,1024]{1,0:T(8,128)(2,1)S(1)} %slice.232), channel_id=1, source_target_pairs={{0,16},{16,0},{1,17},{17,1},{2,18},{18,2},{3,19},{19,3},{4,20},{20... | collective-permute-start | bytes 884744 | tf_op jit(solution)/shard_map/ppermute | solution.py:156
where the time goes:
time: 190 us; the launch traced here: 189 us
  waiting for transfers between devices  77.8 us (41%)
  Pallas kernels  60.4 us (32%)
  starting transfers between devices  42.5 us (22%)
  other arithmetic  4.41 us (2%)
  local copies, waits for them, and re-layouts  3.78 us (2%)
    pallas_call x4, Pallas kernels, ffn(): pl.pallas_call(functools.partial(ffn_kernel, ny, nx, experts, per_group),...  60.4 us
    ppermute x7, waiting for transfers between devices, ring_step(): lax.ppermute(value, 'line', [(order[i], order[(i + 1) % n]) for i in rang...  48.8 us
    ppermute x27, waiting for transfers between devices, shift(): return lax.ppermute(value, axis, [(i, (i + by) % n) for i in range(n)])  29 us
    ppermute x27, starting transfers between devices, shift(): return lax.ppermute(value, axis, [(i, (i + by) % n) for i in range(n)])  28.5 us
    ppermute x7, starting transfers between devices, ring_step(): lax.ppermute(value, 'line', [(order[i], order[(i + 1) % n]) for i in rang...  14.1 us
  transfers between devices with their start and end apart: 34, of which 16 were waited for; matrix products, arithmetic and copies ran while one was open for 4% of the time, Pallas kernels for 32%

commit v1 on v0

--- a/solution.py
+++ b/solution.py
@@ -24,9 +24,9 @@
     weights, refs = refs[:6], refs[6:]
     send_a, keep_a, send_b, keep_b = refs[:4]
     rows, hidden, row_sem = refs[4:]
-    count, depth = rows.shape[0], weights[0].shape[1]
+    count, depth = rows.shape[0], weights[0].shape[0]
     half = depth // 2
-    units = weights[0].shape[0]
+    units = weights[2].shape[0]
     tok = count // (ny * nx)
     group = place[0]
 
@@ -68,22 +68,12 @@
         named.append(0.5 * jnp.sum(jnp.where(pick, extra, 0.0), axis=1, keepdims=True))
 
     per_expert = units // per_group
-    nt = (((1,), (1,)), ((), ()))
     for h in range(2):
         gate, up = weights[3 * h], weights[3 * h + 1]
         for start, size in tiles(units):
-            gate_pre = lax.dot_general(
-                rows[:, :depth],
-                gate[start : start + size],
-                nt,
-                preferred_element_type=jnp.float32,
-            )
-            up_pre = lax.dot_general(
-                rows[:, :depth],
-                up[start : start + size],
-                nt,
-                preferred_element_type=jnp.float32,
-            )
+            cols = slice(start, start + size)
+            gate_pre = jnp.dot(rows[:, :depth], gate[:, cols], preferred_element_type=jnp.float32)
+            up_pre = jnp.dot(rows[:, :depth], up[:, cols], preferred_element_type=jnp.float32)
             low, high = start // per_expert, (start + size - 1) // per_expert
             column = lax.broadcasted_iota(jnp.int32, (1, size), 1) + start
             scale = named[high]
@@ -119,10 +109,29 @@
                         keep_b[there, to] = block
 
 
+def turn_kernel(source, target):
+    for start, size in tiles(source.shape[1]):
+        target[start : start + size, :] = source[:, start : start + size].T
+
+
+def turn(weight):
+    vmem = pl.BlockSpec(memory_space=pltpu.VMEM)
+    return pl.pallas_call(
+        turn_kernel,
+        in_specs=[vmem],
+        out_specs=vmem,
+        out_shape=jax.ShapeDtypeStruct(weight.shape[::-1], weight.dtype),
+        compiler_params=pltpu.CompilerParams(vmem_limit_bytes=16 * 1024 * 1024),
+        cost_estimate=pl.CostEstimate(
+            flops=0, bytes_accessed=4 * weight.size, transcendentals=0
+        ),
+    )(weight)
+
+
 def ffn(first, near, left, right, weights, place, experts, per_group):
     ny, nx = len(left) + 1, len(right) + 1
     tok, width = first.shape
-    units, depth = weights[0].shape
+    units, depth = weights[2].shape
     half, count = depth // 2, ny * nx * tok
     any_spec, vmem = pl.BlockSpec(memory_space=pl.ANY), pl.BlockSpec(memory_space=pltpu.VMEM)
     sources = [first, *near, *left, *right]
@@ -197,8 +206,6 @@
     near = near_of(near)
 
     own = [w.reshape(per_group * units, depth) for w in (gate_weight, up_weight, down_weight)]
-    other = [shift(own[0], "core", 1)]
-
     def add(*terms):
         return sum(t.astype(jnp.float32) for t in terms)
 
@@ -235,9 +242,10 @@
     firsts, nears, sides = [first], [near], [exchange(first, near)]
     firsts.append(ring_step(first))
     nears.append([ring_step(n) for n in near])
-    other.append(shift(after(own[1], other[0], near, firsts[1]), "core", 1))
-    other.append(shift(after(own[2], other[0], near, firsts[1]), "core", 1))
-    weights = own + other
+    own = [turn(own[0]), turn(own[1]), own[2]]
+    other_down = shift(own[2], "core", 1)
+    turned = after(own[:2], other_down, near, firsts[1])
+    weights = own + [shift(w, "core", 1) for w in turned] + [other_down]
 
     parts, begun = {}, {}
     for k in range(1, stages):

time: 190 us -> 221 us (1.16)
  local copies, waits for them, and re-layouts: 3.78 us -> 49.4 us
  waiting for transfers between devices: 77.8 us -> 66.9 us
  starting transfers between devices: 42.5 us -> 36.5 us
  other arithmetic: 4.41 us -> 9.53 us
  Pallas kernels: 60.4 us -> 57 us
    ppermute x7, waiting for transfers between devices: 48.8 us -> 22.7 us  [ring_step(): lax.ppermute(value, 'line', [(order[i], order[(i + 1) % n]) for i in rang...]
    unnamed x13 -> x37, local copies, waits for them, and re-layouts: 0.8 us -> 18.2 us
    ppermute x27, waiting for transfers between devices: 29 us -> 44.2 us  [shift(): return lax.ppermute(value, axis, [(i, (i + by) % n) for i in range(n)])]
    ppermute x0 -> x2, local copies, waits for them, and re-layouts: none -> 9.2 us  [shift(): return lax.ppermute(value, axis, [(i, (i + by) % n) for i in range(n)])]
    optimization_barrier x0 -> x2, local copies, waits for them, and re-layouts: none -> 7.58 us  [after(): return lax.optimization_barrier((value, earlier))[0]]
    pallas_call x4, Pallas kernels: 60.4 us -> 55.3 us  [ffn(): pl.pallas_call(functools.partial(ffn_kernel, ny, nx, experts, per_group),...]
    slice x6, local copies, waits for them, and re-layouts: 0.15 us -> 4.01 us  [halves_of(): return ([n[:, :half] for n in near], [n[:, half:] for n in near])]
    ppermute x7, starting transfers between devices: 14.1 us -> 10.9 us  [ring_step(): lax.ppermute(value, 'line', [(order[i], order[(i + 1) % n]) for i in rang...]
  transfers between devices with their start and end apart: 34 -> 34, of which waited for: 16 -> 17; matrix products, arithmetic and copies ran while one was open for 4% -> 17% of each run, Pallas kernels for 32% -> 26%
where the time goes in v1:
time: 221 us; the launch traced here: 220 us
  waiting for transfers between devices  66.9 us (30%)
  Pallas kernels  57 us (26%)
  local copies, waits for them, and re-layouts  49.4 us (22%)
  starting transfers between devices  36.5 us (17%)
  other arithmetic  9.53 us (4%)
    pallas_call x4, Pallas kernels, ffn(): pl.pallas_call(functools.partial(ffn_kernel, ny, nx, experts, per_group),...  55.3 us
    ppermute x27, waiting for transfers between devices, shift(): return lax.ppermute(value, axis, [(i, (i + by) % n) for i in range(n)])  44.2 us
    ppermute x27, starting transfers between devices, shift(): return lax.ppermute(value, axis, [(i, (i + by) % n) for i in range(n)])  25.6 us
    ppermute x7, waiting for transfers between devices, ring_step(): lax.ppermute(value, 'line', [(order[i], order[(i + 1) % n]) for i in rang...  22.7 us
    unnamed x37, local copies, waits for them, and re-layouts  18.2 us
    ppermute x7, starting transfers between devices, ring_step(): lax.ppermute(value, 'line', [(order[i], order[(i + 1) % n]) for i in rang...  10.9 us
    ppermute x2, local copies, waits for them, and re-layouts, shift(): return lax.ppermute(value, axis, [(i, (i + by) % n) for i in range(n)])  9.2 us
    optimization_barrier x2, local copies, waits for them, and re-layouts, after(): return lax.optimization_barrier((value, earlier))[0]  7.58 us
  transfers between devices with their start and end apart: 34, of which 17 were waited for; matrix products, arithmetic and copies ran while one was open for 17% of the time, Pallas kernels for 26%

profile of v1, /device:TPU:0, one launch (start us, length us, event | category | flops | bytes accessed | tf_op | source)
XLA Modules:
  0.0 219.9 jit_solution(18316064193937732844)
XLA Ops:
  0.5 1.7 slice.135
  2.1 2.6 %collective-permute-start = (bf16[144,1024]{1,0:T(8,128)(2,1)}, bf16[144,1024]{1,0:T(8,128)(2,1)}, u32[]{:S(2)}, u32[]{:S(2)}) collective-permute-start(bf16[144,1024]{1,0:T(8,128)(2,1)} %slice.135), channel_id=1, source_target_pairs={{0,8},{8,0},{1,9},{9,1},{2,10},{10,2},{3,11},{11,3},{4,12},{12,4},... | collective-permute-start | bytes 884744 | tf_op jit(solution)/shard_map/ppermute | solution.py:165
  6.7 1.6 collective-permute-start.4
  9.3 1.6 collective-permute-start.2
  10.9 1.8 copy-done.4
  15.4 1.6 copy-done
  17.1 1.7 constant_dynamic-update-slice_fusion.1
  19.8 4.3 %collective-permute-done.4.refs_1_ = bf16[144,2176]{1,0:T(8,128)(2,1)} collective-permute-done((bf16[144,2176]{1,0:T(8,128)(2,1)}, bf16[144,2176]{1,0:T(8,128)(2,1)}, u32[]{:S(2)}, u32[]{:S(2)}) %collective-permute-start.4) | collective-permute-done | bytes 626720 | tf_op jit(solution)/shard_map/ppermute | solution.py:171
  24.1 4.7 %copy.37 = bf16[2048,704]{0,1:T(8,128)(2,1)} copy(bf16[2048,704]{1,0:T(8,128)(2,1)} %copy-done) | data formatting | bytes 5767168 | tf_op jit(solution)/shard_map/optimization_barrier | solution.py:175
  28.8 2.9 %copy.36 = bf16[2048,704]{0,1:T(8,128)(2,1)} copy(bf16[2048,704]{1,0:T(8,128)(2,1)S(1)} %shard_map.64.refs_6_) | data formatting | bytes 5767168 | tf_op jit(solution)/shard_map/optimization_barrier | solution.py:175
  33.0 1.1 pad_maximum_fusion.4
  34.1 1.6 collective-permute-start.1
  38.4 11.1 %collective-permute-done.5 = bf16[144,2176]{1,0:T(8,128)(2,1)} collective-permute-done((bf16[144,2176]{1,0:T(8,128)(2,1)}, bf16[144,2176]{1,0:T(8,128)(2,1)}, u32[]{:S(2)}, u32[]{:S(2)}) %collective-permute-start.5) | collective-permute-done | bytes 626720 | tf_op jit(solution)/shard_map/ppermute | solution.py:171
  51.4 1.5 collective-permute-start.9
  55.6 2.4 %pad_maximum_fusion = bf16[288,2176]{1,0:T(8,128)(2,1)} fusion(bf16[144,2176]{1,0:T(8,128)(2,1)} %collective-permute-done.5, bf16[144,2176]{1,0:T(8,128)(2,1)} %collective-permute-done.4.refs_1_), kind=kLoop, calls=%fused_computation | loop fusion | flops 2506752 | bytes 2506752 | tf_op jit(solution)/shard_map/concatenate | solution.py:255
  61.0 4.6 %copy.39.refs_10_ = bf16[2048,704]{1,0:T(8,128)(2,1)} copy(bf16[2048,704]{0,1:T(8,128)(2,1)} %collective-permute-done.8) | data formatting | bytes 5767168 | tf_op jit(solution)/shard_map/ppermute | solution.py:165
  65.6 4.6 %copy.38.refs_9_ = bf16[2048,704]{1,0:T(8,128)(2,1)} copy(bf16[2048,704]{0,1:T(8,128)(2,1)} %collective-permute-done.7) | data formatting | bytes 5767168 | tf_op jit(solution)/shard_map/ppermute | solution.py:165
  70.2 1.9 copy-done.1
  72.1 1.9 copy-done.2
  74.0 1.9 copy-done.3
  75.9 1.8 copy-done.10
  79.9 14.2 %shard_map.66 = (bf16[1,288,1024]{2,1,0:T(8,128)(2,1)S(1)}, f32[288,1024]{1,0:T(8,128)S(1)}, bf16[1,288,1024]{2,1,0:T(8,128)(2,1)S(1)}, f32[288,1024]{1,0:T(8,128)S(1)}) custom-call(s32[1]{0:T(128)} %bitcast.refs_0_, bf16[144,2176]{1,0:T(8,128)(2,1)} %concatenate.50.refs_1_, bf16[144,1024]{1,0:T(8,128)(2,1)} %collective-permute-done.refs_2_, ...), custom_call_target="tpu_custom_call" | custom-call | flops 9965666304 | bytes 9437184 | tf_op jit(solution)/shard_map/pallas_call | solution.py:139
  94.1 1.6 collective-permute-start.19
  97.3 1.6 collective-permute-start.17
  98.8 1.1 concatenate.68
  100.6 1.1 slice.173.refs_1_
  101.7 3.6 %collective-permute-start.14 = (bf16[288,2176]{1,0:T(8,128)(2,1)}, bf16[288,2176]{1,0:T(8,128)(2,1)S(1)}, u32[]{:S(2)}, u32[]{:S(2)}) collective-permute-start(bf16[288,2176]{1,0:T(8,128)(2,1)} %collective-permute-done.13), channel_id=1, source_target_pairs={{2,6},{6,4},{4,0},{0,2},{3,7},{7,5},{5,1},{1,3},{10,14},{14,12},{1... | collective-permute-start | bytes 3760136 | tf_op jit(solution)/shard_map/ppermute | solution.py:171
  105.3 5.1 %collective-permute-done.19 = bf16[288,1024]{1,0:T(8,128)(2,1)S(1)} collective-permute-done((bf16[288,1024]{1,0:T(8,128)(2,1)S(1)}, bf16[288,1024]{1,0:T(8,128)(2,1)S(1)}, u32[]{:S(2)}, u32[]{:S(2)}) %collective-permute-start.19) | collective-permute-done | bytes 589856 | tf_op jit(solution)/shard_map/ppermute | solution.py:165
  110.4 1.5 collective-permute-done.11
  111.9 14.5 %shard_map.67 = (bf16[1,288,1024]{2,1,0:T(8,128)(2,1)S(1)}, f32[288,1024]{1,0:T(8,128)S(1)}, bf16[1,288,1024]{2,1,0:T(8,128)(2,1)S(1)}, f32[288,1024]{1,0:T(8,128)S(1)}) custom-call(s32[1]{0:T(128)} %bitcast.refs_0_, bf16[144,2176]{1,0:T(8,128)(2,1)} %collective-permute-done.4.refs_1_, bf16[144,1024]{1,0:T(8,128)(2,1)S(1)} %copy-done.9, ...), custom_call_target="tpu_custom_call" | custom-call | flops 9965666304 | bytes 9437184 | tf_op jit(solution)/shard_map/pallas_call | solution.py:139
  129.9 1.3 collective-permute-start.15
  131.2 1.6 collective-permute-start.16
  132.9 9.8 %collective-permute-done.21 = bf16[288,1024]{1,0:T(8,128)(2,1)S(1)} collective-permute-done((bf16[288,1024]{1,0:T(8,128)(2,1)S(1)}, bf16[288,1024]{1,0:T(8,128)(2,1)S(1)}, u32[]{:S(2)}, u32[]{:S(2)}) %collective-permute-start.21) | collective-permute-done | bytes 589856 | tf_op jit(solution)/shard_map/ppermute | solution.py:165
  143.2 3.4 %collective-permute-start.26 = (bf16[288,2048]{1,0:T(8,128)(2,1)S(1)}, bf16[288,2048]{1,0:T(8,128)(2,1)S(1)}, u32[]{:S(2)}, u32[]{:S(2)}) collective-permute-start(bf16[288,2048]{1,0:T(8,128)(2,1)S(1)} %pad_maximum_fusion.1), channel_id=1, source_target_pairs={{2,6},{6,4},{4,0},{0,2},{3,7},{7,5},{5,1},{1,3},{10,14},{14,12},{1... | collective-permute-start | bytes 3538952 | tf_op jit(solution)/shard_map/ppermute | solution.py:171
  146.6 13.2 %shard_map.68 = (bf16[1,288,1024]{2,1,0:T(8,128)(2,1)S(1)}, f32[288,1024]{1,0:T(8,128)S(1)}, bf16[1,288,1024]{2,1,0:T(8,128)(2,1)S(1)}, f32[288,1024]{1,0:T(8,128)S(1)}) custom-call(s32[1]{0:T(128)} %bitcast.refs_0_, bf16[144,2176]{1,0:T(8,128)(2,1)S(1)} %slice.173.refs_1_, bf16[144,1024]{1,0:T(8,128)(2,1)S(1)} %slice.174.refs_2_, ...), custom_call_target="tpu_custom_call" | custom-call | flops 9965666304 | bytes 9437184 | tf_op jit(solution)/shard_map/pallas_call | solution.py:139
  159.9 1.2 collective-permute-start.23
  161.6 13.4 %shard_map.69 = (bf16[1,288,1024]{2,1,0:T(8,128)(2,1)S(1)}, f32[288,1024]{1,0:T(8,128)S(1)}, bf16[1,288,1024]{2,1,0:T(8,128)(2,1)S(1)}, f32[288,1024]{1,0:T(8,128)S(1)}) custom-call(s32[1]{0:T(128)} %bitcast.refs_0_, bf16[144,2176]{1,0:T(8,128)(2,1)S(1)} %slice.172.refs_1_, bf16[144,1024]{1,0:T(8,128)(2,1)S(1)} %slice.176.refs_2_, ...), custom_call_target="tpu_custom_call" | custom-call | flops 9965666304 | bytes 9437184 | tf_op jit(solution)/shard_map/pallas_call | solution.py:139
  175.3 1.9 collective-permute-done.22
  178.4 2.1 collective-permute-start.28
  180.5 1.6 collective-permute-start.27
  182.1 8.4 %collective-permute-done.30 = bf16[288,1024]{1,0:T(8,128)(2,1)S(1)} collective-permute-done((bf16[288,1024]{1,0:T(8,128)(2,1)S(1)}, bf16[288,1024]{1,0:T(8,128)(2,1)S(1)}, u32[]{:S(2)}, u32[]{:S(2)}) %collective-permute-start.30) | collective-permute-done | bytes 589856 | tf_op jit(solution)/shard_map/ppermute | solution.py:165
  190.8 2.0 collective-permute-done.28
  192.9 3.7 %collective-permute-done.27 = bf16[144,1024]{1,0:T(8,128)(2,1)S(1)} collective-permute-done((bf16[144,1024]{1,0:T(8,128)(2,1)S(1)}, bf16[144,1024]{1,0:T(8,128)(2,1)S(1)}, u32[]{:S(2)}, u32[]{:S(2)}) %collective-permute-start.27) | collective-permute-done | bytes 294944 | tf_op jit(solution)/shard_map/ppermute | solution.py:165
  197.9 2.1 collective-permute-start.12
  200.1 4.3 %collective-permute-done.25 = bf16[144,1024]{1,0:T(8,128)(2,1)S(1)} collective-permute-done((bf16[144,1024]{1,0:T(8,128)(2,1)S(1)}, bf16[144,1024]{1,0:T(8,128)(2,1)S(1)}, u32[]{:S(2)}, u32[]{:S(2)}) %collective-permute-start.25) | collective-permute-done | bytes 294944 | tf_op jit(solution)/shard_map/ppermute | solution.py:165
  204.4 3.2 %collective-permute-done.29 = bf16[144,2048]{1,0:T(8,128)(2,1)S(1)} collective-permute-done((bf16[144,2048]{1,0:T(8,128)(2,1)S(1)}, bf16[144,2048]{1,0:T(8,128)(2,1)S(1)}, u32[]{:S(2)}, u32[]{:S(2)}) %collective-permute-start.29) | collective-permute-done | bytes 589856 | tf_op jit(solution)/shard_map/ppermute | solution.py:171
  208.3 6.7 %collective-permute-done.33 = bf16[144,1024]{1,0:T(8,128)(2,1)S(1)} collective-permute-done((bf16[144,1024]{1,0:T(8,128)(2,1)S(1)}, bf16[144,1024]{1,0:T(8,128)(2,1)S(1)}, u32[]{:S(2)}, u32[]{:S(2)}) %collective-permute-start.33) | collective-permute-done | bytes 294944 | tf_op jit(solution)/shard_map/ppermute | solution.py:165
  215.0 3.8 %collective-permute-done.32 = bf16[144,2048]{1,0:T(8,128)(2,1)S(1)} collective-permute-done((bf16[144,2048]{1,0:T(8,128)(2,1)S(1)}, bf16[144,2048]{1,0:T(8,128)(2,1)S(1)}, u32[]{:S(2)}, u32[]{:S(2)}) %collective-permute-start.32) | collective-permute-done | bytes 589856 | tf_op jit(solution)/shard_map/ppermute | solution.py:171
  (117 shorter events, 32.4 us)
Async XLA Ops:
  0.0 5.7 %copy-start.17 = (bf16[144,2048]{1,0:T(8,128)(2,1)S(1)}, bf16[144,2048]{1,0:T(8,128)(2,1)}, u32[]{:S(2)}) copy-start(bf16[144,2048]{1,0:T(8,128)(2,1)} %param.6) | copy-start | bytes 1769476
  0.0 24.1 %collective-permute-start.6 = (bf16[704,2048]{1,0:T(8,128)(2,1)}, bf16[704,2048]{1,0:T(8,128)(2,1)}, u32[]{:S(2)}, u32[]{:S(2)}) collective-permute-start(bf16[704,2048]{1,0:T(8,128)(2,1)} %bitcast.14), channel_id=1, source_target_pairs={{0,1},{1,0},{2,3},{3,2},{4,5},{5,4},{6,7},{7,6},{8,9},{9,8},{10,11... | collective-permute-start | bytes 8650760 | tf_op jit(solution)/shard_map/ppermute | solution.py:165
  2.1 14.9 %collective-permute-start = (bf16[144,1024]{1,0:T(8,128)(2,1)}, bf16[144,1024]{1,0:T(8,128)(2,1)}, u32[]{:S(2)}, u32[]{:S(2)}) collective-permute-start(bf16[144,1024]{1,0:T(8,128)(2,1)} %slice.135), channel_id=1, source_target_pairs={{0,8},{8,0},{1,9},{9,1},{2,10},{10,2},{3,11},{11,3},{4,12},{12,4},... | collective-permute-start | bytes 884744 | tf_op jit(solution)/shard_map/ppermute | solution.py:165
  6.7 17.4 %collective-permute-start.4 = (bf16[144,2176]{1,0:T(8,128)(2,1)}, bf16[144,2176]{1,0:T(8,128)(2,1)}, u32[]{:S(2)}, u32[]{:S(2)}) collective-permute-start(bf16[144,2176]{1,0:T(8,128)(2,1)} %concatenate.50.refs_1_), channel_id=1, source_target_pairs={{2,6},{6,4},{4,0},{0,2},{3,7},{7,5},{5,1},{1,3},{10,14},{14,12},{1... | collective-permute-start | bytes 1880072 | tf_op jit(solution)/shard_map/ppermute | solution.py:171
  9.3 4.3 %copy-start.15 = (bf16[144,1152]{1,0:T(8,128)(2,1)}, bf16[144,1152]{1,0:T(8,128)(2,1)S(1)}, u32[]{:S(2)}) copy-start(bf16[144,1152]{1,0:T(8,128)(2,1)S(1)} %slice.165) | copy-start | bytes 995332
  9.3 9.6 %collective-permute-start.2 = (bf16[144,1152]{1,0:T(8,128)(2,1)S(1)}, bf16[144,1152]{1,0:T(8,128)(2,1)S(1)}, u32[]{:S(2)}, u32[]{:S(2)}) collective-permute-start(bf16[144,1152]{1,0:T(8,128)(2,1)S(1)} %slice.165), channel_id=1, source_target_pairs={{0,16},{16,0},{1,17},{17,1},{2,18},{18,2},{3,19},{19,3},{4,20},{20... | collective-permute-start | bytes 995336 | tf_op jit(solution)/shard_map/ppermute | solution.py:165
  10.9 1.8 copy-start.4
  12.7 1.8 copy-start.5
  15.4 1.6 copy-start
  28.8 32.2 %collective-permute-start.8 = (bf16[2048,704]{0,1:T(8,128)(2,1)}, bf16[2048,704]{0,1:T(8,128)(2,1)}, u32[]{:S(2)}, u32[]{:S(2)}) collective-permute-start(bf16[2048,704]{0,1:T(8,128)(2,1)} %copy.37), channel_id=1, source_target_pairs={{0,1},{1,0},{2,3},{3,2},{4,5},{5,4},{6,7},{7,6},{8,9},{9,8},{10,11... | collective-permute-start | bytes 8650760 | tf_op jit(solution)/shard_map/ppermute | solution.py:165
  31.7 34.0 %collective-permute-start.7 = (bf16[2048,704]{0,1:T(8,128)(2,1)}, bf16[2048,704]{0,1:T(8,128)(2,1)}, u32[]{:S(2)}, u32[]{:S(2)}) collective-permute-start(bf16[2048,704]{0,1:T(8,128)(2,1)} %copy.36), channel_id=1, source_target_pairs={{0,1},{1,0},{2,3},{3,2},{4,5},{5,4},{6,7},{7,6},{8,9},{9,8},{10,11... | collective-permute-start | bytes 8650760 | tf_op jit(solution)/shard_map/ppermute | solution.py:165
  32.2 17.2 %collective-permute-start.5 = (bf16[144,2176]{1,0:T(8,128)(2,1)}, bf16[144,2176]{1,0:T(8,128)(2,1)}, u32[]{:S(2)}, u32[]{:S(2)}) collective-permute-start(bf16[144,2176]{1,0:T(8,128)(2,1)} %constant_dynamic-update-slice_fusion), channel_id=1, source_target_pairs={{2,6},{6,4},{4,0},{0,2},{3,7},{7,5},{5,1},{1,3},{10,14},{14,12},{1... | collective-permute-start | bytes 1880072 | tf_op jit(solution)/shard_map/ppermute | solution.py:171
  33.0 2.7 %copy-start.16 = (bf16[144,1152]{1,0:T(8,128)(2,1)S(1)}, bf16[144,1152]{1,0:T(8,128)(2,1)}, u32[]{:S(2)}) copy-start(bf16[144,1152]{1,0:T(8,128)(2,1)} %copy-done.15) | copy-start | bytes 995332
  34.1 23.9 %collective-permute-start.1 = (bf16[288,1024]{1,0:T(8,128)(2,1)S(1)}, bf16[288,1024]{1,0:T(8,128)(2,1)S(1)}, u32[]{:S(2)}, u32[]{:S(2)}) collective-permute-start(bf16[288,1024]{1,0:T(8,128)(2,1)S(1)} %pad_maximum_fusion.4), channel_id=1, source_target_pairs={{0,16},{16,0},{1,17},{17,1},{2,18},{18,2},{3,19},{19,3},{4,20},{20... | collective-permute-start | bytes 1769480 | tf_op jit(solution)/shard_map/ppermute | solution.py:165
  35.8 23.6 %collective-permute-start.3 = (bf16[288,1152]{1,0:T(8,128)(2,1)S(1)}, bf16[288,1152]{1,0:T(8,128)(2,1)S(1)}, u32[]{:S(2)}, u32[]{:S(2)}) collective-permute-start(bf16[288,1152]{1,0:T(8,128)(2,1)S(1)} %pad_maximum_fusion.2), channel_id=1, source_target_pairs={{0,8},{8,0},{1,9},{9,1},{2,10},{10,2},{3,11},{11,3},{4,12},{12,4},... | collective-permute-start | bytes 1990664 | tf_op jit(solution)/shard_map/ppermute | solution.py:165
  51.4 42.7 %collective-permute-start.9 = (bf16[288,1024]{1,0:T(8,128)(2,1)}, bf16[288,1024]{1,0:T(8,128)(2,1)}, u32[]{:S(2)}, u32[]{:S(2)}) collective-permute-start(bf16[288,1024]{1,0:T(8,128)(2,1)} %pad_maximum_fusion.5), channel_id=1, source_target_pairs={{0,16},{16,0},{1,17},{17,1},{2,18},{18,2},{3,19},{19,3},{4,20},{20... | collective-permute-start | bytes 1769480 | tf_op jit(solution)/shard_map/ppermute | solution.py:165
  58.8 35.2 %collective-permute-start.10 = (bf16[288,1152]{1,0:T(8,128)(2,1)}, bf16[288,1152]{1,0:T(8,128)(2,1)}, u32[]{:S(2)}, u32[]{:S(2)}) collective-permute-start(bf16[288,1152]{1,0:T(8,128)(2,1)} %pad_maximum_fusion.3), channel_id=1, source_target_pairs={{0,8},{8,0},{1,9},{9,1},{2,10},{10,2},{3,11},{11,3},{4,12},{12,4},... | collective-permute-start | bytes 1990664 | tf_op jit(solution)/shard_map/ppermute | solution.py:165
  60.2 35.9 %collective-permute-start.13 = (bf16[288,2176]{1,0:T(8,128)(2,1)}, bf16[288,2176]{1,0:T(8,128)(2,1)}, u32[]{:S(2)}, u32[]{:S(2)}) collective-permute-start(bf16[288,2176]{1,0:T(8,128)(2,1)} %pad_maximum_fusion), channel_id=1, source_target_pairs={{2,6},{6,4},{4,0},{0,2},{3,7},{7,5},{5,1},{1,3},{10,14},{14,12},{1... | collective-permute-start | bytes 3760136 | tf_op jit(solution)/shard_map/ppermute | solution.py:171
  70.2 1.9 copy-start.1
  72.1 1.9 copy-start.2
  74.0 1.9 copy-start.3
  75.9 1.8 copy-start.10
  77.7 1.1 copy-start.12
  78.8 1.1 copy-start.14
  94.1 16.3 %collective-permute-start.19 = (bf16[288,1024]{1,0:T(8,128)(2,1)S(1)}, bf16[288,1024]{1,0:T(8,128)(2,1)S(1)}, u32[]{:S(2)}, u32[]{:S(2)}) collective-permute-start(bf16[288,1024]{1,0:T(8,128)(2,1)S(1)} %bitcast.24), channel_id=1, source_target_pairs={{0,8},{8,0},{1,9},{9,1},{2,10},{10,2},{3,11},{11,3},{4,12},{12,4},... | collective-permute-start | bytes 1769480 | tf_op jit(solution)/shard_map/ppermute | solution.py:165
  95.6 16.3 %collective-permute-start.11 = (bf16[288,1024]{1,0:T(8,128)(2,1)S(1)}, bf16[288,1024]{1,0:T(8,128)(2,1)S(1)}, u32[]{:S(2)}, u32[]{:S(2)}) collective-permute-start(bf16[288,1024]{1,0:T(8,128)(2,1)S(1)} %bitcast.22), channel_id=1, source_target_pairs={{0,16},{16,0},{1,17},{17,1},{2,18},{18,2},{3,19},{19,3},{4,20},{20... | collective-permute-start | bytes 1769480 | tf_op jit(solution)/shard_map/ppermute | solution.py:165
  97.2 14.7 %copy-start.7 = (bf16[144,1152]{1,0:T(8,128)(2,1)S(1)}, bf16[144,1152]{1,0:T(8,128)(2,1)}, u32[]{:S(2)}) copy-start(bf16[144,1152]{1,0:T(8,128)(2,1)} %copy-done.6) | copy-start | bytes 995332
  97.2 14.6 %copy-start.9 = (bf16[144,1024]{1,0:T(8,128)(2,1)S(1)}, bf16[144,1024]{1,0:T(8,128)(2,1)}, u32[]{:S(2)}) copy-start(bf16[144,1024]{1,0:T(8,128)(2,1)} %copy-done.8) | copy-start | bytes 884740
  97.3 29.1 %collective-permute-start.17 = (bf16[288,1024]{1,0:T(8,128)(2,1)S(1)}, bf16[288,1024]{1,0:T(8,128)(2,1)S(1)}, u32[]{:S(2)}, u32[]{:S(2)}) collective-permute-start(bf16[288,1024]{1,0:T(8,128)(2,1)S(1)} %concatenate.67), channel_id=1, source_target_pairs={{0,16},{16,0},{1,17},{17,1},{2,18},{18,2},{3,19},{19,3},{4,20},{20... | collective-permute-start | bytes 1769480 | tf_op jit(solution)/shard_map/ppermute | solution.py:165
  100.0 26.4 %collective-permute-start.18 = (bf16[288,1152]{1,0:T(8,128)(2,1)S(1)}, bf16[288,1152]{1,0:T(8,128)(2,1)S(1)}, u32[]{:S(2)}, u32[]{:S(2)}) collective-permute-start(bf16[288,1152]{1,0:T(8,128)(2,1)S(1)} %concatenate.68), channel_id=1, source_target_pairs={{0,8},{8,0},{1,9},{9,1},{2,10},{10,2},{3,11},{11,3},{4,12},{12,4},... | collective-permute-start | bytes 1990664 | tf_op jit(solution)/shard_map/ppermute | solution.py:165
  101.7 28.1 %collective-permute-start.14 = (bf16[288,2176]{1,0:T(8,128)(2,1)}, bf16[288,2176]{1,0:T(8,128)(2,1)S(1)}, u32[]{:S(2)}, u32[]{:S(2)}) collective-permute-start(bf16[288,2176]{1,0:T(8,128)(2,1)} %collective-permute-done.13), channel_id=1, source_target_pairs={{2,6},{6,4},{4,0},{0,2},{3,7},{7,5},{5,1},{1,3},{10,14},{14,12},{1... | collective-permute-start | bytes 3760136 | tf_op jit(solution)/shard_map/ppermute | solution.py:171
  126.4 16.3 %collective-permute-start.21 = (bf16[288,1024]{1,0:T(8,128)(2,1)S(1)}, bf16[288,1024]{1,0:T(8,128)(2,1)S(1)}, u32[]{:S(2)}, u32[]{:S(2)}) collective-permute-start(bf16[288,1024]{1,0:T(8,128)(2,1)S(1)} %bitcast.23), channel_id=1, source_target_pairs={{0,8},{8,0},{1,9},{9,1},{2,10},{10,2},{3,11},{11,3},{4,12},{12,4},... | collective-permute-start | bytes 1769480 | tf_op jit(solution)/shard_map/ppermute | solution.py:165
  127.0 15.7 %collective-permute-start.20 = (bf16[288,1024]{1,0:T(8,128)(2,1)S(1)}, bf16[288,1024]{1,0:T(8,128)(2,1)S(1)}, u32[]{:S(2)}, u32[]{:S(2)}) collective-permute-start(bf16[288,1024]{1,0:T(8,128)(2,1)S(1)} %bitcast.21), channel_id=1, source_target_pairs={{0,16},{16,0},{1,17},{17,1},{2,18},{18,2},{3,19},{19,3},{4,20},{20... | collective-permute-start | bytes 1769480 | tf_op jit(solution)/shard_map/ppermute | solution.py:165
  129.9 30.0 %collective-permute-start.15 = (bf16[288,1024]{1,0:T(8,128)(2,1)S(1)}, bf16[288,1024]{1,0:T(8,128)(2,1)S(1)}, u32[]{:S(2)}, u32[]{:S(2)}) collective-permute-start(bf16[288,1024]{1,0:T(8,128)(2,1)S(1)} %concatenate.65), channel_id=1, source_target_pairs={{0,16},{16,0},{1,17},{17,1},{2,18},{18,2},{3,19},{19,3},{4,20},{20... | collective-permute-start | bytes 1769480 | tf_op jit(solution)/shard_map/ppermute | solution.py:165
  131.2 28.7 %collective-permute-start.16 = (bf16[288,1152]{1,0:T(8,128)(2,1)S(1)}, bf16[288,1152]{1,0:T(8,128)(2,1)S(1)}, u32[]{:S(2)}, u32[]{:S(2)}) collective-permute-start(bf16[288,1152]{1,0:T(8,128)(2,1)S(1)} %concatenate.66), channel_id=1, source_target_pairs={{0,8},{8,0},{1,9},{9,1},{2,10},{10,2},{3,11},{11,3},{4,12},{12,4},... | collective-permute-start | bytes 1990664 | tf_op jit(solution)/shard_map/ppermute | solution.py:165
  143.2 34.5 %collective-permute-start.26 = (bf16[288,2048]{1,0:T(8,128)(2,1)S(1)}, bf16[288,2048]{1,0:T(8,128)(2,1)S(1)}, u32[]{:S(2)}, u32[]{:S(2)}) collective-permute-start(bf16[288,2048]{1,0:T(8,128)(2,1)S(1)} %pad_maximum_fusion.1), channel_id=1, source_target_pairs={{2,6},{6,4},{4,0},{0,2},{3,7},{7,5},{5,1},{1,3},{10,14},{14,12},{1... | collective-permute-start | bytes 3538952 | tf_op jit(solution)/shard_map/ppermute | solution.py:171
  159.9 15.5 %collective-permute-start.23 = (bf16[288,1024]{1,0:T(8,128)(2,1)S(1)}, bf16[288,1024]{1,0:T(8,128)(2,1)S(1)}, u32[]{:S(2)}, u32[]{:S(2)}) collective-permute-start(bf16[288,1024]{1,0:T(8,128)(2,1)S(1)} %bitcast.26), channel_id=1, source_target_pairs={{0,8},{8,0},{1,9},{9,1},{2,10},{10,2},{3,11},{11,3},{4,12},{12,4},... | collective-permute-start | bytes 1769480 | tf_op jit(solution)/shard_map/ppermute | solution.py:165
  161.1 16.2 %collective-permute-start.22 = (bf16[288,1024]{1,0:T(8,128)(2,1)S(1)}, bf16[288,1024]{1,0:T(8,128)(2,1)S(1)}, u32[]{:S(2)}, u32[]{:S(2)}) collective-permute-start(bf16[288,1024]{1,0:T(8,128)(2,1)S(1)} %bitcast.25), channel_id=1, source_target_pairs={{0,16},{16,0},{1,17},{17,1},{2,18},{18,2},{3,19},{19,3},{4,20},{20... | collective-permute-start | bytes 1769480 | tf_op jit(solution)/shard_map/ppermute | solution.py:165
  177.3 13.3 %collective-permute-start.30 = (bf16[288,1024]{1,0:T(8,128)(2,1)S(1)}, bf16[288,1024]{1,0:T(8,128)(2,1)S(1)}, u32[]{:S(2)}, u32[]{:S(2)}) collective-permute-start(bf16[288,1024]{1,0:T(8,128)(2,1)S(1)} %bitcast.20), channel_id=1, source_target_pairs={{0,8},{8,0},{1,9},{9,1},{2,10},{10,2},{3,11},{11,3},{4,12},{12,4},... | collective-permute-start | bytes 1769480 | tf_op jit(solution)/shard_map/ppermute | solution.py:165
  177.7 19.7 %collective-permute-start.24 = (bf16[288,1024]{1,0:T(8,128)(2,1)S(1)}, bf16[288,1024]{1,0:T(8,128)(2,1)S(1)}, u32[]{:S(2)}, u32[]{:S(2)}) collective-permute-start(bf16[288,1024]{1,0:T(8,128)(2,1)S(1)} %bitcast.19), channel_id=1, source_target_pairs={{0,16},{16,0},{1,17},{17,1},{2,18},{18,2},{3,19},{19,3},{4,20},{20... | collective-permute-start | bytes 1769480 | tf_op jit(solution)/shard_map/ppermute | solution.py:165
  178.4 14.5 %collective-permute-start.28 = (bf16[144,1024]{1,0:T(8,128)(2,1)S(1)}, bf16[144,1024]{1,0:T(8,128)(2,1)S(1)}, u32[]{:S(2)}, u32[]{:S(2)}) collective-permute-start(bf16[144,1024]{1,0:T(8,128)(2,1)S(1)} %slice.234), channel_id=1, source_target_pairs={{0,16},{16,0},{1,17},{17,1},{2,18},{18,2},{3,19},{19,3},{4,20},{20... | collective-permute-start | bytes 884744 | tf_op jit(solution)/shard_map/ppermute | solution.py:165
  180.5 16.2 %collective-permute-start.27 = (bf16[144,1024]{1,0:T(8,128)(2,1)S(1)}, bf16[144,1024]{1,0:T(8,128)(2,1)S(1)}, u32[]{:S(2)}, u32[]{:S(2)}) collective-permute-start(bf16[144,1024]{1,0:T(8,128)(2,1)S(1)} %slice.235), channel_id=1, source_target_pairs={{0,8},{8,0},{1,9},{9,1},{2,10},{10,2},{3,11},{11,3},{4,12},{12,4},... | collective-permute-start | bytes 884744 | tf_op jit(solution)/shard_map/ppermute | solution.py:165
  190.7 9.4 %collective-permute-start.31 = (bf16[144,1024]{1,0:T(8,128)(2,1)S(1)}, bf16[144,1024]{1,0:T(8,128)(2,1)S(1)}, u32[]{:S(2)}, u32[]{:S(2)}) collective-permute-start(bf16[144,1024]{1,0:T(8,128)(2,1)S(1)} %slice.233), channel_id=1, source_target_pairs={{0,16},{16,0},{1,17},{17,1},{2,18},{18,2},{3,19},{19,3},{4,20},{20... | collective-permute-start | bytes 884744 | tf_op jit(solution)/shard_map/ppermute | solution.py:165
  196.8 10.8 %collective-permute-start.29 = (bf16[144,2048]{1,0:T(8,128)(2,1)S(1)}, bf16[144,2048]{1,0:T(8,128)(2,1)S(1)}, u32[]{:S(2)}, u32[]{:S(2)}) collective-permute-start(bf16[144,2048]{1,0:T(8,128)(2,1)S(1)} %pad_maximum_fusion.6), channel_id=1, source_target_pairs={{2,6},{6,4},{4,0},{0,2},{3,7},{7,5},{5,1},{1,3},{10,14},{14,12},{1... | collective-permute-start | bytes 1769480 | tf_op jit(solution)/shard_map/ppermute | solution.py:171
  197.6 6.8 %collective-permute-start.25 = (bf16[144,1024]{1,0:T(8,128)(2,1)S(1)}, bf16[144,1024]{1,0:T(8,128)(2,1)S(1)}, u32[]{:S(2)}, u32[]{:S(2)}) collective-permute-start(bf16[144,1024]{1,0:T(8,128)(2,1)S(1)} %slice.236), channel_id=1, source_target_pairs={{0,8},{8,0},{1,9},{9,1},{2,10},{10,2},{3,11},{11,3},{4,12},{12,4},... | collective-permute-start | bytes 884744 | tf_op jit(solution)/shard_map/ppermute | solution.py:165
  197.9 10.4 %collective-permute-start.12 = (bf16[144,1024]{1,0:T(8,128)(2,1)S(1)}, bf16[144,1024]{1,0:T(8,128)(2,1)S(1)}, u32[]{:S(2)}, u32[]{:S(2)}) collective-permute-start(bf16[144,1024]{1,0:T(8,128)(2,1)S(1)} %slice.237), channel_id=1, source_target_pairs={{0,8},{8,0},{1,9},{9,1},{2,10},{10,2},{3,11},{11,3},{4,12},{12,4},... | collective-permute-start | bytes 884744 | tf_op jit(solution)/shard_map/ppermute | solution.py:165
  207.9 10.8 %collective-permute-start.32 = (bf16[144,2048]{1,0:T(8,128)(2,1)S(1)}, bf16[144,2048]{1,0:T(8,128)(2,1)S(1)}, u32[]{:S(2)}, u32[]{:S(2)}) collective-permute-start(bf16[144,2048]{1,0:T(8,128)(2,1)S(1)} %pad_maximum_fusion.7), channel_id=1, source_target_pairs={{2,6},{6,4},{4,0},{0,2},{3,7},{7,5},{5,1},{1,3},{10,14},{14,12},{1... | collective-permute-start | bytes 1769480 | tf_op jit(solution)/shard_map/ppermute | solution.py:171
  208.2 6.8 %collective-permute-start.33 = (bf16[144,1024]{1,0:T(8,128)(2,1)S(1)}, bf16[144,1024]{1,0:T(8,128)(2,1)S(1)}, u32[]{:S(2)}, u32[]{:S(2)}) collective-permute-start(bf16[144,1024]{1,0:T(8,128)(2,1)S(1)} %slice.232), channel_id=1, source_target_pairs={{0,16},{16,0},{1,17},{17,1},{2,18},{18,2},{3,19},{19,3},{4,20},{20... | collective-permute-start | bytes 884744 | tf_op jit(solution)/shard_map/ppermute | solution.py:165
  (4 other events, 3.4 us)
